TPU v7x, 256 devices: a whole 4x4x8 slice. The times are simulated.
256 devices in a mesh: island: 2 (over core), tensor: 32 (over y, z_lo, x), fsdp: 4 (over z_hi).
Axes of the slice: x: 4, y: 4, z: 8 (z_hi: 4, z_lo: 2; z = z_hi * 2 + z_lo), core: 2. Of those that a mesh axis runs over, the one named last changes fastest.
Arguments:
- tokens: bfloat16 [8, 3584, 1792], P(('island', 'fsdp'), 'tensor'), may hold values from -6 to 6
- hidden_cot: bfloat16 [8, 3584, 8192], P(('island', 'fsdp'), None, 'tensor'), may hold values from -6 to 6
- inner_gate: float32 [2, 1792, 8192], P('island', 'fsdp', 'tensor'), may hold values from -6 to 6
- inner_up: float32 [2, 1792, 8192], P('island', 'fsdp', 'tensor'), may hold values from -6 to 6
- moment_gate: float32 [2, 1792, 8192], P('island', 'fsdp', 'tensor'), may hold values from -4 to 4
- moment_up: float32 [2, 1792, 8192], P('island', 'fsdp', 'tensor'), may hold values from -4 to 4
- second_gate: float32 [2, 1792, 8192], P('island', 'fsdp', 'tensor'), may hold values from 0.01 to 1
- second_up: float32 [2, 1792, 8192], P('island', 'fsdp', 'tensor'), may hold values from 0.01 to 1
- outer_gate: float32 [1792, 8192], P('fsdp', 'tensor'), may hold values from -6 to 6
- outer_up: float32 [1792, 8192], P('fsdp', 'tensor'), may hold values from -6 to 6
- velocity_gate: float32 [1792, 8192], P('fsdp', 'tensor'), may hold values from -4 to 4
- velocity_up: float32 [1792, 8192], P('fsdp', 'tensor'), may hold values from -4 to 4
- step_count: int32 [1], replicated, may hold values from 1 to 39
Outputs:
- new_outer_gate: float32 [1792, 8192], P('fsdp', 'tensor')
- new_outer_up: float32 [1792, 8192], P('fsdp', 'tensor')
- new_velocity_gate: float32 [1792, 8192], P('fsdp', 'tensor')
- new_velocity_up: float32 [1792, 8192], P('fsdp', 'tensor')
All inputs are finite; a program needn't handle non-finite values.
Results may differ from a plain program's by a relative error of at most 0.00065.
Values may be sent and summed in bfloat16 or wider, within the bound.
No kernel may reach another device: no remote copies, remote signals or barrier semaphores. Data moves between devices by JAX's collectives and lax.ppermute only.
A program may use at most 192 MiB of HBM per device.

v0:
```python
import math

import jax
import jax.numpy as jnp
from jax import lax
from jax.sharding import PartitionSpec as P

D = 1792


beta_first = 0.9
beta_second = 0.95
adam_eps = 1e-08
inner_rate = 0.03
decay_rate = 0.1
outer_momentum = 0.9
outer_rate = 0.7


def adam_update(gradient, first, second, corr_first, corr_second):
    first_new = beta_first * first + (1.0 - beta_first) * gradient
    second_new = beta_second * second + (1.0 - beta_second) * gradient * gradient
    return first_new / corr_first / (jnp.sqrt(second_new / corr_second) + adam_eps)


def outer_apply(outer, velocity, summed, islands):
    mean_delta = summed / float(islands)
    velocity_new = outer_momentum * velocity + mean_delta
    return (outer - outer_rate * (mean_delta + outer_momentum * velocity_new), velocity_new)


def shards(
    tokens,
    hidden_cot,
    inner_gate,
    inner_up,
    moment_gate,
    moment_up,
    second_gate,
    second_up,
    outer_gate,
    outer_up,
    velocity_gate,
    velocity_up,
    step_count,
):
    islands = lax.axis_size("island")
    scale_in = D ** (-0.5)
    param_gate = inner_gate[0]
    param_up = inner_up[0]
    hidden_cols = param_gate.shape[1]
    full_x = lax.all_gather(tokens[0], "tensor", axis=0, tiled=True)
    cot_rows = hidden_cot[0].astype(jnp.float32)
    local_weights = jnp.concatenate(
        [param_gate.astype(jnp.bfloat16), param_up.astype(jnp.bfloat16)], axis=1
    )
    pair_weights = lax.all_gather(local_weights, "fsdp", axis=0, tiled=True)
    projected = jnp.dot(full_x, pair_weights, preferred_element_type=jnp.float32) * scale_in
    gate = projected[:, :hidden_cols]
    upval = projected[:, hidden_cols:]
    sigmoid_gate = jax.nn.sigmoid(gate)
    dgate = (cot_rows * upval * sigmoid_gate * (1.0 + gate * (1.0 - sigmoid_gate))).astype(
        jnp.bfloat16
    )
    dup = (cot_rows * gate * sigmoid_gate).astype(jnp.bfloat16)
    pair_grads = jnp.concatenate([dgate, dup], axis=1)
    weight_grad = lax.psum_scatter(
        (
            lax.dot_general(
                full_x, pair_grads, (((0,), (0,)), ((), ())), preferred_element_type=jnp.float32
            )
            * scale_in
        ).astype(jnp.bfloat16),
        "fsdp",
        scatter_dimension=0,
        tiled=True,
    ).astype(jnp.float32)
    step_float = step_count[0].astype(jnp.float32)
    corr_first = 1.0 - jnp.exp(step_float * math.log(beta_first))
    corr_second = 1.0 - jnp.exp(step_float * math.log(beta_second))
    update_gate = adam_update(
        weight_grad[:, :hidden_cols], moment_gate[0], second_gate[0], corr_first, corr_second
    )
    update_up = adam_update(
        weight_grad[:, hidden_cols:], moment_up[0], second_up[0], corr_first, corr_second
    )
    new_gate = param_gate - inner_rate * (update_gate + decay_rate * param_gate)
    new_up = param_up - inner_rate * (update_up + decay_rate * param_up)
    summed_gate, summed_up = lax.psum((outer_gate - new_gate, outer_up - new_up), "island")
    out_gate, vel_gate = outer_apply(outer_gate, velocity_gate, summed_gate, islands)
    out_up, vel_up = outer_apply(outer_up, velocity_up, summed_up, islands)
    return (out_gate, out_up, vel_gate, vel_up)


def solution(mesh):
    return jax.shard_map(
        shards,
        mesh=mesh,
        in_specs=(
            P(("island", "fsdp"), "tensor", None),
            P(("island", "fsdp"), None, "tensor"),
            P("island", "fsdp", "tensor"),
            P("island", "fsdp", "tensor"),
            P("island", "fsdp", "tensor"),
            P("island", "fsdp", "tensor"),
            P("island", "fsdp", "tensor"),
            P("island", "fsdp", "tensor"),
            P("fsdp", "tensor"),
            P("fsdp", "tensor"),
            P("fsdp", "tensor"),
            P("fsdp", "tensor"),
            P(),
        ),
        out_specs=(
            P("fsdp", "tensor"),
            P("fsdp", "tensor"),
            P("fsdp", "tensor"),
            P("fsdp", "tensor"),
        ),
        check_vma=False,
    )
```

profile of v0, /device:TPU:1, one launch (start us, length us, event | category | flops | bytes accessed | tf_op | source)
XLA Modules:
  0.0 358.0 jit_solution(12610261807036207794)
XLA Ops:
  7.2 0.0 all-gather.4.cloned.1.call-start
  7.2 1.2 bitcast_convert_fusion
  8.4 0.8 pad_maximum_fusion
  9.2 0.0 all-gather.4.cloned.1.call-update
  9.2 0.0 all-gather.6.cloned.1.call-start
  9.3 0.7 all-gather.6.cloned.1.call-update
  10.0 0.0 reduce-scatter.4.cloned.1.call-start
  10.0 2.8 copy.34
  12.8 48.0 %all-gather.4.cloned.1.call-done = bf16[1792,512]{1,0:T(8,128)(2,1)} async-done(((bf16[448,512]{1,0:T(8,128)(2,1)}), bf16[1792,512]{1,0:T(8,128)(2,1)}) %all-gather.4.cloned.1.call-update) | async-done | bytes 1835024 | tf_op jit(solution)/shard_map/all_gather | solution.py:57
  60.8 165.0 %all-gather.6.cloned.1.call-done = bf16[1,3584,1792]{2,1,0:T(8,128)(2,1)} async-done(((bf16[1,112,1792]{2,1,0:T(8,128)(2,1)}), bf16[1,3584,1792]{2,1,0:T(8,128)(2,1)}) %all-gather.6.cloned.1.call-update) | async-done | bytes 12845072 | tf_op jit(solution)/shard_map/all_gather | solution.py:52
  225.7 10.4 %multiply_bitcast_fusion = f32[3584,512]{0,1:T(8,128)S(1)} fusion(bf16[1792,512]{1,0:T(8,128)(2,1)} %all-gather.4.cloned.1.call-done, bf16[1,3584,1792]{2,1,0:T(8,128)(2,1)} %all-gather.6.cloned.1.call-done), kind=kOutput, calls=%fused_computation.4 | convolution fusion | flops 6578503680 | bytes 22020096 | tf_op jit(solution)/shard_map/dot_general | solution.py:58
  236.2 1.7 fusion.8
  237.9 11.8 %fusion.18 = bf16[1792,512]{0,1:T(8,128)(2,1)} fusion(bf16[1,3584,1792]{2,1,0:T(8,128)(2,1)} %all-gather.6.cloned.1.call-done, bf16[3584,256]{0,1:T(8,128)(2,1)S(1)} %get-tuple-element.15, bf16[3584,256]{0,1:T(8,128)(2,1)S(1)} %get-tuple-element.14), kind=kOutput, calls=%fused_computation.17 | convolution fusion | flops 6585843712 | bytes 18350080 | tf_op jit(solution)/shard_map/dot_general | solution.py:69
  249.7 0.0 copy-start
  249.7 0.0 copy-start.1
  249.7 0.0 copy-start.2
  249.7 0.0 copy-start.3
  249.7 0.0 copy-start.4
  249.8 0.0 copy-start.5
  249.8 0.0 copy-start.6
  249.8 4.0 %copy.36 = bf16[1792,512]{1,0:T(8,128)(2,1)} copy(bf16[1792,512]{0,1:T(8,128)(2,1)} %fusion.18) | data formatting | bytes 3670016
  253.8 0.0 reduce-scatter.4.cloned.1.call-update
  253.8 0.0 all-reduce.3.cloned.1.call-start
  254.6 59.4 %reduce-scatter.4.cloned.1.call-done = bf16[448,512]{1,0:T(8,128)(2,1)} async-done(((bf16[1792,512]{1,0:T(8,128)(2,1)}), bf16[448,512]{1,0:T(8,128)(2,1)}) %reduce-scatter.4.cloned.1.call-update) | async-done | bytes 458768 | tf_op jit(solution)/shard_map/reduce_scatter | solution.py:67
  314.0 1.1 convert_element_type.39
  315.1 0.0 copy-done
  315.1 0.0 copy-done.1
  315.1 0.0 copy-done.2
  315.1 0.0 copy-done.3
  315.2 0.0 copy-done.4
  315.2 0.0 copy-done.5
  315.2 0.0 copy-done.6
  315.2 2.7 fusion.37
  317.9 0.0 all-reduce.3.cloned.1.call-update
  317.9 29.1 %all-reduce.3.cloned.1.call-done = (f32[448,256]{1,0:T(8,128)}, f32[448,256]{1,0:T(8,128)}) async-done(((f32[448,256]{1,0:T(8,128)}, f32[448,256]{1,0:T(8,128)}), (f32[448,256]{1,0:T(8,128)}, f32[448,256]{1,0:T(8,128)})) %all-reduce.3.cloned.1.call-update) | async-done | bytes 917520 | tf_op jit(solution)/shard_map/psum | solution.py:89
  347.1 2.2 multiply_subtract_fusion
  349.3 2.2 multiply_subtract_fusion.1
Async XLA Ops:
  7.2 53.6 %all-gather.4.cloned.1.call-start = ((), (), s32[]{:S(2)}) async-start(), calls=%async_computation.1 | async-start | bytes 2293760 | tf_op jit(solution)/shard_map/all_gather | solution.py:57
  9.2 216.5 %all-gather.6.cloned.1.call-start = ((), (), s32[]{:S(2)}) async-start(), calls=%async_computation.2 | async-start | bytes 13246464 | tf_op jit(solution)/shard_map/all_gather | solution.py:52
  10.0 304.0 %reduce-scatter.4.cloned.1.call-start = ((), (), s32[]{:S(2)}) async-start(), calls=%async_computation.3 | async-start | bytes 2293760 | tf_op jit(solution)/shard_map/reduce_scatter | solution.py:67
  249.7 65.4 %copy-start = (f32[1,448,256]{2,1,0:T(8,128)S(1)}, f32[1,448,256]{2,1,0:T(8,128)}, u32[]{:S(2)}) copy-start(f32[1,448,256]{2,1,0:T(8,128)} %param.16) | copy-start | bytes 1376260
  249.7 65.4 %copy-start.1 = (f32[1,448,256]{2,1,0:T(8,128)S(1)}, f32[1,448,256]{2,1,0:T(8,128)}, u32[]{:S(2)}) copy-start(f32[1,448,256]{2,1,0:T(8,128)} %param.15) | copy-start | bytes 1376260
  249.7 65.4 %copy-start.2 = (f32[448,256]{1,0:T(8,128)S(1)}, f32[448,256]{1,0:T(8,128)}, u32[]{:S(2)}) copy-start(f32[448,256]{1,0:T(8,128)} %param.22) | copy-start | bytes 1376260
  249.7 65.4 %copy-start.3 = (f32[448,256]{1,0:T(8,128)S(1)}, f32[448,256]{1,0:T(8,128)}, u32[]{:S(2)}) copy-start(f32[448,256]{1,0:T(8,128)} %param.21) | copy-start | bytes 1376260
  249.7 65.4 %copy-start.4 = (f32[1,448,256]{2,1,0:T(8,128)S(1)}, f32[1,448,256]{2,1,0:T(8,128)}, u32[]{:S(2)}) copy-start(f32[1,448,256]{2,1,0:T(8,128)} %param.20) | copy-start | bytes 1376260
  249.8 65.4 %copy-start.5 = (f32[1,448,256]{2,1,0:T(8,128)S(1)}, f32[1,448,256]{2,1,0:T(8,128)}, u32[]{:S(2)}) copy-start(f32[1,448,256]{2,1,0:T(8,128)} %param.18) | copy-start | bytes 1376260
  249.8 65.4 %copy-start.6 = (f32[1,448,256]{2,1,0:T(8,128)S(1)}, f32[1,448,256]{2,1,0:T(8,128)}, u32[]{:S(2)}) copy-start(f32[1,448,256]{2,1,0:T(8,128)} %param.19) | copy-start | bytes 1376260
  253.8 93.3 %all-reduce.3.cloned.1.call-start = ((), (), s32[]{:S(2)}) async-start(), calls=%async_computation.4 | async-start | bytes 1835008 | tf_op jit(solution)/shard_map/psum | solution.py:89
Sparse Core Ops, SparseCore 0:
  10.4 50.3 all-gather.3
  62.6 163.1 all-gather.5
  253.9 60.0 reduce-scatter.3
  318.0 28.9 all-reduce.2
where the time goes:
time: 358 us
  waiting for transfers between devices  302 us (84%)
  matrix products  22.2 us (6%)
  between operations  14.6 us (4%)
  other arithmetic  12 us (3%)
  local copies, waits for them, and re-layouts  6.77 us (2%)
    all_gather x1, waiting for transfers between devices, shards(): full_x = lax.all_gather(tokens[0], 'tensor', axis=0, tiled=True)  165 us
    reduce_scatter x1, waiting for transfers between devices, shards(): lax.psum_scatter((lax.dot_general(full_x, pair_grads, (((0,), (0,)), ((),...  59.4 us
    all_gather x1, waiting for transfers between devices, shards(): pair_weights = lax.all_gather(local_weights, 'fsdp', axis=0, tiled=True)  48 us
    psum x1, waiting for transfers between devices, shards(): lax.psum((outer_gate - new_gate, outer_up - new_up), 'island')  29.1 us
    dot_general x1, matrix products, shards(): lax.dot_general(full_x, pair_grads, (((0,), (0,)), ((), ())), preferred_e...  11.8 us
    dot_general x1, matrix products, shards(): jnp.dot(full_x, pair_weights, preferred_element_type=jnp.float32) * scale_in  10.4 us
  transfers between devices with their start and end apart: 4, of which 4 were waited for; matrix products, arithmetic and copies ran while one was open for 1% of the time, Pallas kernels for 0%

commit v1 on v0

v1 whole, which is shorter than its diff:
```python
import functools
import math

import jax
import jax.numpy as jnp
from jax import lax
from jax.experimental import pallas as pl
from jax.experimental.pallas import tpu as pltpu
from jax.sharding import PartitionSpec as P

beta_first = 0.9
beta_second = 0.95
adam_eps = 1e-08
inner_rate = 0.03
decay_rate = 0.1
outer_momentum = 0.9
outer_rate = 0.7

AXES = ("island", "tensor", "fsdp")
NX, NY, NL, NH = 4, 4, 2, 4


def route(target):
    pairs = []
    for c in range(2):
        for y in range(NY):
            for l in range(NL):
                for x in range(NX):
                    for h in range(NH):
                        dc, dy, dl, dx, dh = target(c, y, l, x, h)
                        src = (c * 32 + y * 8 + l * 4 + x) * 4 + h
                        dst = (dc * 32 + (dy % NY) * 8 + dl * 4 + dx % NX) * 4 + dh % NH
                        pairs.append((src, dst))
    return pairs


def send(block, target):
    return lax.ppermute(block, AXES, route(target))


def swap_hop(step):
    return lambda c, y, l, x, h: (l, y, c, x, h + step)


def high_hop(step):
    return lambda c, y, l, x, h: (c, y, l, x, h + step)


def first_hop(step):
    return lambda c, y, l, x, h: (c, y, l, x + step, h) if c == 0 else (c, y + step, l, x, h)


def second_hop(step):
    return lambda c, y, l, x, h: (c, y + step, l, x, h) if c == 0 else (c, y, l, x + step, h)


def core_hop(c, y, l, x, h):
    return (1 - c, y, l, x, h)


def block_kernel(layout, n_weights, final, scale, *refs):
    index_ref, refs = refs[0], refs[1:]
    weight_refs, refs = refs[:n_weights], refs[n_weights:]
    cot_ref, refs = refs[0], refs[1:]
    n_x = 1 + max(op for piece in layout for op, _, _ in piece)
    x_refs, refs = refs[:n_x], refs[n_x:]
    if final:
        given_ref, refs = refs[0], refs[1:]
        outs, refs = refs[:7], refs[7:]
        total, refs = refs[0], refs[1:]
    else:
        total, refs = refs[0], refs[1:]
    xbuf, gbuf, wbuf, pbuf, dbuf, xsem, gsem, wsem, tsem = refs
    n_pieces = len(layout)
    rows = xbuf.shape[1]
    feats = wbuf.shape[0]
    shard = feats // NH
    half = shard // 2
    cols = pbuf.shape[1] // 2
    per = gbuf.shape[1]
    high = index_ref[index_ref.shape[0] - 1]

    def fetch(piece, slot):
        for k in range(n_pieces):

            @pl.when(piece == k)
            def _(k=k):
                for op, first, count in layout[k]:
                    pltpu.make_async_copy(
                        x_refs[op], xbuf.at[slot, pl.ds(first, count)], xsem.at[slot]
                    ).start()

        for q in range(per):
            pltpu.make_async_copy(
                cot_ref.at[index_ref[piece * per + q]], gbuf.at[slot, q], gsem.at[slot]
            ).start()

    spots = ((0, 0), (1, 0), (2, 0), (2, 1), (3, 0))
    for ref, (ahead, part) in zip(weight_refs, spots):
        at = lax.rem(high + ahead, NH) * shard + part * half
        pltpu.make_async_copy(ref, wbuf.at[pl.ds(pl.multiple_of(at, 16), ref.shape[0])], wsem).start()
    fetch(0, 0)
    if final:
        pltpu.make_async_copy(given_ref, total, tsem).start()
    pltpu.make_async_copy(wbuf, wbuf, wsem).wait()

    def one(piece, carry):
        slot = lax.rem(piece, 2)

        @pl.when(piece + 1 < n_pieces)
        def _():
            fetch(piece + 1, 1 - slot)

        pltpu.make_async_copy(xbuf.at[slot], xbuf.at[slot], xsem.at[slot]).wait()
        pltpu.make_async_copy(gbuf.at[slot], gbuf.at[slot], gsem.at[slot]).wait()
        x = xbuf[slot]
        pbuf[...] = jnp.dot(x, wbuf[...], preferred_element_type=jnp.float32)
        tok = rows // per
        for q in range(per):
            at = pl.ds(q * tok, tok)
            gate = pbuf[at, :cols] * scale
            upval = pbuf[at, cols:] * scale
            cot = gbuf[slot, q].astype(jnp.float32)
            s = jax.nn.sigmoid(gate)
            cs = cot * s
            dbuf[at, :cols] = (cs * upval * (1.0 + gate * (1.0 - s))).astype(jnp.bfloat16)
            dbuf[at, cols:] = (cs * gate).astype(jnp.bfloat16)
        if final:

            @pl.when(piece == 0)
            def _():
                pltpu.make_async_copy(given_ref, total, tsem).wait()

        grad = lax.dot_general(
            x, dbuf[...], (((0,), (0,)), ((), ())), preferred_element_type=jnp.float32
        )
        if final:
            total[...] += grad
        else:

            @pl.when(piece == 0)
            def _():
                total[...] = grad

            @pl.when(piece > 0)
            def _():
                total[...] += grad

        return carry

    lax.fori_loop(0, n_pieces, one, 0)
    if final:

        def rounded(ahead, first, count):
            at = lax.rem(high + ahead, NH) * shard + first
            return (total[pl.ds(pl.multiple_of(at, 16), count), :] * scale).astype(jnp.bfloat16)

        opp_a, opp_b, up_a, up_b, down_a, down_b, own = outs
        opp_a[...] = rounded(2, 0, half)
        opp_b[...] = rounded(2, half, half)
        up_a[...] = rounded(1, 0, half)
        up_b[...] = rounded(1, half, half)
        down_a[...] = rounded(3, 0, half)
        down_b[...] = rounded(3, half, half)
        own[...] = rounded(0, 0, shard)


def blocks(index, weights, cot, xs, layout, given, scale):
    shard, wide = weights[0].shape
    feats = shard * NH
    per = 4
    rows = per * cot.shape[1]
    cols = wide // 2
    final = given is not None
    hbm = pl.BlockSpec(memory_space=pl.ANY)
    vmem = pl.BlockSpec(memory_space=pltpu.VMEM)
    operands = [index, *weights, cot, *xs]
    in_specs = [pl.BlockSpec(memory_space=pltpu.SMEM)] + [hbm] * (len(operands) - 1)
    scratch = []
    if final:
        operands.append(given)
        in_specs.append(hbm)
        half = jax.ShapeDtypeStruct((shard // 2, wide), jnp.bfloat16)
        out_shape = [half] * 6 + [jax.ShapeDtypeStruct((shard, wide), jnp.bfloat16)]
        out_specs = [vmem] * 7
        scratch.append(pltpu.VMEM((feats, wide), jnp.float32))
    else:
        out_shape = jax.ShapeDtypeStruct((feats, wide), jnp.float32)
        out_specs = vmem
    scratch += [
        pltpu.VMEM((2, rows, feats), jnp.bfloat16),
        pltpu.VMEM((2, per, cot.shape[1], cols), jnp.bfloat16),
        pltpu.VMEM((feats, wide), jnp.bfloat16),
        pltpu.VMEM((rows, wide), jnp.float32),
        pltpu.VMEM((rows, wide), jnp.bfloat16),
        pltpu.SemaphoreType.DMA((2,)),
        pltpu.SemaphoreType.DMA((2,)),
        pltpu.SemaphoreType.DMA,
        pltpu.SemaphoreType.DMA,
    ]
    flops = 4 * len(layout) * rows * feats * wide
    return pl.pallas_call(
        functools.partial(block_kernel, layout, len(weights), final, scale),
        out_shape=out_shape,
        in_specs=in_specs,
        out_specs=out_specs,
        scratch_shapes=scratch,
        cost_estimate=pl.CostEstimate(
            flops=flops, bytes_accessed=len(layout) * rows * feats * 2, transcendentals=0
        ),
        compiler_params=pltpu.CompilerParams(vmem_limit_bytes=40 * 1024 * 1024),
    )(*operands)


def shards(
    tokens,
    hidden_cot,
    inner_gate,
    inner_up,
    moment_gate,
    moment_up,
    second_gate,
    second_up,
    outer_gate,
    outer_up,
    velocity_gate,
    velocity_up,
    step_count,
):
    islands = float(lax.axis_size("island"))
    feats = tokens.shape[2]
    scale = feats ** (-0.5)
    core = lax.axis_index("island")
    place = lax.axis_index("tensor")
    high = lax.axis_index("fsdp")
    y, x = place // 8, place % 4
    tok = tokens.shape[1]
    shard, cols = inner_gate.shape[1:]
    half = shard // 2

    mine = send(tokens[0], swap_hop(0))
    local = jnp.concatenate([inner_gate[0], inner_up[0]], axis=1)
    local_low = local.astype(jnp.bfloat16)
    w_own = send(local_low, swap_hop(0))
    w_prev = send(local_low, swap_hop(1))
    w_next = send(local_low, swap_hop(-1))
    w_far_a = send(w_prev[:half], high_hop(1))
    w_far_b = send(w_next[half:], high_hop(-1))
    weights = [w_own, w_next, w_far_a, w_far_b, w_prev]

    before = send(mine, first_hop(1))
    after = send(mine, first_hop(-1))
    cut = tok // 2
    far_a = send(before[:cut], first_hop(1))
    far_b = send(after[cut:], first_hop(-1))
    line = jnp.concatenate([mine, before, after, far_a, far_b], axis=0)
    line_before = send(line, second_hop(1))
    line_after = send(line, second_hop(-1))
    cut = 2 * tok
    line_far_a = send(line_before[:cut], second_hop(1))
    line_far_b = send(line_after[cut:], second_hop(-1))
    line_o = send(line, core_hop)
    line_before_o = send(line_before, core_hop)
    line_after_o = send(line_after, core_hop)
    line_far_a_o = send(line_far_a, core_hop)
    line_far_b_o = send(line_far_b, core_hop)

    cot = send(hidden_cot[0], swap_hop(0)).reshape(-1, tok, cols)
    index = []
    for across in (0, -1, 1, 2):
        for lineage in (core, 1 - core):
            for along in (0, -1, 1, 2):
                sy = jnp.where(lineage == 0, y + across, y + along) % NY
                sx = jnp.where(lineage == 0, x + along, x + across) % NX
                index.append(sy * 8 + lineage * 4 + sx)
    index_early = jnp.stack(index[:24] + [high]).astype(jnp.int32)
    index_late = jnp.stack(index[24:] + [high]).astype(jnp.int32)
    rows = 4 * tok
    early = blocks(
        index_early,
        weights,
        cot,
        [line, line_o, line_before, line_before_o, line_after, line_after_o],
        [[(k, 0, rows)] for k in range(6)],
        None,
        scale,
    )
    opp_a, opp_b, up_a, up_b, down_a, down_b, own = blocks(
        index_late,
        weights,
        cot,
        [line_far_a, line_far_b, line_far_a_o, line_far_b_o],
        [[(0, 0, cut), (1, cut, cut)], [(2, 0, cut), (3, cut, cut)]],
        early,
        scale,
    )

    got_a = send(opp_a, high_hop(1))
    got_b = send(opp_b, high_hop(-1))
    from_prev_b = send(up_b, swap_hop(1))
    from_next_a = send(down_a, swap_hop(-1))
    from_own = send(own, swap_hop(0))

    def plus(a, b):
        return (a.astype(jnp.float32) + b.astype(jnp.float32)).astype(jnp.bfloat16)

    from_prev_a = send(plus(up_a, got_a), swap_hop(1))
    from_next_b = send(plus(down_b, got_b), swap_hop(-1))
    f32 = jnp.float32
    from_own = from_own.astype(f32)
    grad = jnp.concatenate(
        [
            from_own[:half] + from_prev_a.astype(f32) + from_next_a.astype(f32),
            from_own[half:] + from_prev_b.astype(f32) + from_next_b.astype(f32),
        ],
        axis=0,
    )

    step_float = step_count[0].astype(jnp.float32)
    corr_first = 1.0 - jnp.exp(step_float * math.log(beta_first))
    corr_second = 1.0 - jnp.exp(step_float * math.log(beta_second))

    def update(gradient, first, second):
        first_new = beta_first * first + (1.0 - beta_first) * gradient
        second_new = beta_second * second + (1.0 - beta_second) * gradient * gradient
        return first_new / corr_first / (jnp.sqrt(second_new / corr_second) + adam_eps)

    def rest(outer, param):
        return outer - (1.0 - inner_rate * decay_rate) * param

    rest_gate, rest_up = rest(outer_gate, inner_gate[0]), rest(outer_up, inner_up[0])
    rest_gate = rest_gate + send(rest_gate, core_hop)
    rest_up = rest_up + send(rest_up, core_hop)
    new_gate = update(grad[:, :cols], moment_gate[0], second_gate[0])
    new_up = update(grad[:, cols:], moment_up[0], second_up[0])
    new_gate = new_gate + send(new_gate, core_hop)
    new_up = new_up + send(new_up, core_hop)

    def apply(outer, velocity, fixed, change):
        mean_delta = (fixed + inner_rate * change) / islands
        velocity_new = outer_momentum * velocity + mean_delta
        return outer - outer_rate * (mean_delta + outer_momentum * velocity_new), velocity_new

    out_gate, vel_gate = apply(outer_gate, velocity_gate, rest_gate, new_gate)
    out_up, vel_up = apply(outer_up, velocity_up, rest_up, new_up)
    return (out_gate, out_up, vel_gate, vel_up)


def solution(mesh):
    state = P("island", "fsdp", "tensor")
    param = P("fsdp", "tensor")
    return jax.shard_map(
        shards,
        mesh=mesh,
        in_specs=(
            P(("island", "fsdp"), "tensor", None),
            P(("island", "fsdp"), None, "tensor"),
            *[state] * 6,
            *[param] * 4,
            P(),
        ),
        out_specs=(param,) * 4,
        check_vma=False,
    )
```

time: 358 us -> 201 us (0.56)
  waiting for transfers between devices: 302 us -> 81.7 us
  starting transfers between devices: 0.16 us -> 63.7 us
  Pallas kernels: 0 us -> 29.9 us
  matrix products: 22.2 us -> 0 us
  between operations: 14.6 us -> 1.78 us
  local copies, waits for them, and re-layouts: 6.77 us -> 17.4 us
  other arithmetic: 12 us -> 3.41 us
    all_gather x2 -> x0, waiting for transfers between devices: 213 us -> none  [the longest x1 165 us: shards(): full_x = lax.all_gather(tokens[0], 'tensor', axis=0, tiled=True)]
    ppermute x0 -> x31, waiting for transfers between devices: none -> 81.7 us  [send(): return lax.ppermute(block, AXES, route(target))]
    ppermute x0 -> x31, starting transfers between devices: none -> 63.7 us  [send(): return lax.ppermute(block, AXES, route(target))]
    reduce_scatter x1 -> x0, waiting for transfers between devices: 59.4 us -> none  [shards(): lax.psum_scatter((lax.dot_general(full_x, pair_grads, (((0,), (0,)), ((),...]
    pallas_call x0 -> x2, Pallas kernels: none -> 29.9 us  [blocks(): pl.pallas_call(functools.partial(block_kernel, layout, len(weights), fina...]
    psum x1 -> x0, waiting for transfers between devices: 29.1 us -> none  [shards(): lax.psum((outer_gate - new_gate, outer_up - new_up), 'island')]
    dot_general x2 -> x0, matrix products: 22.2 us -> none  [the longest x1 11.8 us: shards(): lax.dot_general(full_x, pair_grads, (((0,), (0,)), ((), ())), preferred_e...]
    unnamed x16 -> x58, local copies, waits for them, and re-layouts: 6.77 us -> 14.5 us
  transfers between devices with their start and end apart: 4 -> 31, of which waited for: 4 -> 14; matrix products, arithmetic and copies ran while one was open for 1% -> 4% of each run, Pallas kernels for 0% -> 11%
where the time goes in v1:
time: 201 us; the launch traced here: 198 us
  waiting for transfers between devices  81.7 us (41%)
  starting transfers between devices  63.7 us (32%)
  Pallas kernels  29.9 us (15%)
  local copies, waits for them, and re-layouts  17.4 us (9%)
  other arithmetic  3.41 us (2%)
    ppermute x31, waiting for transfers between devices, send(): return lax.ppermute(block, AXES, route(target))  81.7 us
    ppermute x31, starting transfers between devices, send(): return lax.ppermute(block, AXES, route(target))  63.7 us
    pallas_call x2, Pallas kernels, blocks(): pl.pallas_call(functools.partial(block_kernel, layout, len(weights), fina...  29.9 us
    unnamed x58, local copies, waits for them, and re-layouts  14.5 us
  transfers between devices with their start and end apart: 31, of which 14 were waited for; matrix products, arithmetic and copies ran while one was open for 4% of the time, Pallas kernels for 11%

profile of v1, /device:TPU:1, one launch (start us, length us, event | category | flops | bytes accessed | tf_op | source)
XLA Modules:
  0.0 197.9 jit_solution(16444943102367132303)
XLA Ops:
  0.6 4.9 %collective-permute-start.7 = (bf16[112,1792]{1,0:T(8,128)(2,1)}, bf16[112,1792]{1,0:T(8,128)(2,1)S(1)}, u32[]{:S(2)}, u32[]{:S(2)}) collective-permute-start(bf16[112,1792]{1,0:T(8,128)(2,1)} %bitcast.61), channel_id=1, source_target_pairs={{0,0},{1,1},{2,2},{3,3},{4,4},{5,5},{6,6},{7,7},{8,8},{9,9},{10,10... | collective-permute-start | bytes 1204232 | tf_op jit(solution)/shard_map/ppermute | solution.py:38
  5.6 6.0 %collective-permute-done.7 = bf16[112,1792]{1,0:T(8,128)(2,1)S(1)} collective-permute-done((bf16[112,1792]{1,0:T(8,128)(2,1)}, bf16[112,1792]{1,0:T(8,128)(2,1)S(1)}, u32[]{:S(2)}, u32[]{:S(2)}) %collective-permute-start.7) | collective-permute-done | bytes 401440 | tf_op jit(solution)/shard_map/ppermute | solution.py:38
  11.6 1.3 collective-permute-start.8
  12.9 1.4 collective-permute-start.9
  14.3 0.8 constant_dynamic-update-slice_fusion.4
  15.1 4.8 %collective-permute-done.8 = bf16[112,1792]{1,0:T(8,128)(2,1)S(1)} collective-permute-done((bf16[112,1792]{1,0:T(8,128)(2,1)S(1)}, bf16[112,1792]{1,0:T(8,128)(2,1)S(1)}, u32[]{:S(2)}, u32[]{:S(2)}) %collective-permute-start.8) | collective-permute-done | bytes 401440 | tf_op jit(solution)/shard_map/ppermute | solution.py:38
  19.9 0.1 collective-permute-start.10
  20.0 2.7 %collective-permute-start.11 = (bf16[56,1792]{1,0:T(8,128)(2,1)S(1)}, bf16[56,1792]{1,0:T(8,128)(2,1)S(1)}, u32[]{:S(2)}, u32[]{:S(2)}) collective-permute-start(bf16[56,1792]{1,0:T(8,128)(2,1)S(1)} %slice.43), channel_id=1, source_target_pairs={{0,12},{1,13},{2,14},{3,15},{4,0},{5,1},{6,2},{7,3},{8,4},{9,5},{1... | collective-permute-start | bytes 602120 | tf_op jit(solution)/shard_map/ppermute | solution.py:38
  22.8 0.8 constant_dynamic-update-slice_fusion.3
  23.5 0.8 constant_dynamic-update-slice_fusion.2
  24.3 1.4 collective-permute-done.10
  25.8 0.7 constant_dynamic-update-slice_fusion.1
  26.5 0.7 constant_dynamic-update-slice_fusion.refs_7_
  27.2 2.0 %collective-permute-start.12 = (bf16[448,1792]{1,0:T(8,128)(2,1)}, bf16[448,1792]{1,0:T(8,128)(2,1)S(1)}, u32[]{:S(2)}, u32[]{:S(2)}) collective-permute-start(bf16[448,1792]{1,0:T(8,128)(2,1)} %constant_dynamic-update-slice_fusion.refs_7_), channel_id=1, source_target_pairs={{0,32},{1,33},{2,34},{3,35},{4,36},{5,37},{6,38},{7,39},{8,40},{9,... | collective-permute-start | bytes 4816904 | tf_op jit(solution)/shard_map/ppermute | solution.py:38
  29.2 0.7 collective-permute-start.14
  29.9 8.1 %collective-permute-start.6 = (bf16[3584,256]{1,0:T(8,128)(2,1)S(1)}, bf16[3584,256]{1,0:T(8,128)(2,1)S(1)}, u32[]{:S(2)}, u32[]{:S(2)}) collective-permute-start(bf16[3584,256]{1,0:T(8,128)(2,1)S(1)} %bitcast.60), channel_id=1, source_target_pairs={{0,0},{1,1},{2,2},{3,3},{4,4},{5,5},{6,6},{7,7},{8,8},{9,9},{10,10... | collective-permute-start | bytes 5505032 | tf_op jit(solution)/shard_map/ppermute | solution.py:38
  38.0 2.8 %collective-permute-start.3 = (bf16[448,512]{1,0:T(8,128)(2,1)S(1)}, bf16[448,512]{1,0:T(8,128)(2,1)S(1)}, u32[]{:S(2)}, u32[]{:S(2)}) collective-permute-start(bf16[448,512]{1,0:T(8,128)(2,1)S(1)} %pad_maximum_fusion.1), channel_id=1, source_target_pairs={{0,1},{1,2},{2,3},{3,0},{4,5},{5,6},{6,7},{7,4},{8,9},{9,10},{10,1... | collective-permute-start | bytes 1376264 | tf_op jit(solution)/shard_map/ppermute | solution.py:38
  40.8 1.3 collective-permute-start.2
  42.2 20.8 %collective-permute-done.3.refs_5_ = bf16[448,512]{1,0:T(8,128)(2,1)S(1)} collective-permute-done((bf16[448,512]{1,0:T(8,128)(2,1)S(1)}, bf16[448,512]{1,0:T(8,128)(2,1)S(1)}, u32[]{:S(2)}, u32[]{:S(2)}) %collective-permute-start.3) | collective-permute-done | bytes 458784 | tf_op jit(solution)/shard_map/ppermute | solution.py:38
  63.0 14.1 %collective-permute-start.1 = (bf16[448,512]{1,0:T(8,128)(2,1)S(1)}, bf16[448,512]{1,0:T(8,128)(2,1)S(1)}, u32[]{:S(2)}, u32[]{:S(2)}) collective-permute-start(bf16[448,512]{1,0:T(8,128)(2,1)S(1)} %pad_maximum_fusion.1), channel_id=1, source_target_pairs={{0,0},{1,1},{2,2},{3,3},{4,4},{5,5},{6,6},{7,7},{8,8},{9,9},{10,10... | collective-permute-start | bytes 1376264 | tf_op jit(solution)/shard_map/ppermute | solution.py:38
  77.3 0.5 collective-permute-start.19
  77.7 0.1 collective-permute-start.20
  77.9 0.8 copy-done
  78.6 8.8 %collective-permute-done.1.refs_1_ = bf16[448,512]{1,0:T(8,128)(2,1)S(1)} collective-permute-done((bf16[448,512]{1,0:T(8,128)(2,1)S(1)}, bf16[448,512]{1,0:T(8,128)(2,1)S(1)}, u32[]{:S(2)}, u32[]{:S(2)}) %collective-permute-start.1) | collective-permute-done | bytes 458784 | tf_op jit(solution)/shard_map/ppermute | solution.py:38
  87.5 0.7 copy-done.9
  88.2 8.7 %collective-permute-done.4.refs_3_ = bf16[224,512]{1,0:T(8,128)(2,1)S(1)} collective-permute-done((bf16[224,512]{1,0:T(8,128)(2,1)S(1)}, bf16[224,512]{1,0:T(8,128)(2,1)S(1)}, u32[]{:S(2)}, u32[]{:S(2)}) %collective-permute-start.4) | collective-permute-done | bytes 229408 | tf_op jit(solution)/shard_map/ppermute | solution.py:38
  96.9 1.0 slice.44
  97.9 0.9 slice.45
  98.8 4.2 %collective-permute-done.5.refs_4_ = bf16[224,512]{1,0:T(8,128)(2,1)S(1)} collective-permute-done((bf16[224,512]{1,0:T(8,128)(2,1)S(1)}, bf16[224,512]{1,0:T(8,128)(2,1)S(1)}, u32[]{:S(2)}, u32[]{:S(2)}) %collective-permute-start.5) | collective-permute-done | bytes 229408 | tf_op jit(solution)/shard_map/ppermute | solution.py:38
  103.1 0.7 copy-done.11
  103.8 1.3 copy-done.6
  105.0 2.7 %collective-permute-start.15 = (bf16[224,1792]{1,0:T(8,128)(2,1)}, bf16[224,1792]{1,0:T(8,128)(2,1)}, u32[]{:S(2)}, u32[]{:S(2)}) collective-permute-start(bf16[224,1792]{1,0:T(8,128)(2,1)} %slice.45), channel_id=1, source_target_pairs={{0,96},{1,97},{2,98},{3,99},{4,100},{5,101},{6,102},{7,103},{8,104... | collective-permute-start | bytes 2408456 | tf_op jit(solution)/shard_map/ppermute | solution.py:38
  107.8 0.1 stack.140.refs_0_
  107.9 8.4 %collective-permute-done.13.refs_7_ = bf16[224,1792]{1,0:T(8,128)(2,1)} collective-permute-done((bf16[224,1792]{1,0:T(8,128)(2,1)}, bf16[224,1792]{1,0:T(8,128)(2,1)}, u32[]{:S(2)}, u32[]{:S(2)}) %collective-permute-start.13) | collective-permute-done | bytes 802848 | tf_op jit(solution)/shard_map/ppermute | solution.py:38
  116.3 0.8 collective-permute-done.15.refs_8_
  117.2 1.0 copy-done.1
  118.2 1.0 copy-done.4
  119.2 1.5 copy-done.7
  120.7 1.0 copy-done.10
  121.7 0.9 copy-done.12
  122.7 21.6 %shard_map.156.refs_11_ = f32[1792,512]{1,0:T(8,128)} custom-call(s32[25]{0:T(128)S(1)} %stack.140.refs_0_, bf16[448,512]{1,0:T(8,128)(2,1)S(1)} %copy-done.10, bf16[448,512]{1,0:T(8,128)(2,1)S(1)} %copy-done.4, bf16[224,512]{1,0:T(8,128)(2,1)S(1)} %collective-permute-done.4.refs_3_, bf16[224,512]{1,0:T(8,128)(2,1)S(1)} %copy-done.12, ...), custom_call_target="tpu_custom_call" | custom-call | flops 9865003008 | bytes 9633792 | tf_op jit(solution)/shard_map/pallas_call | solution.py:202
  144.3 2.0 %copy-done.13 = f32[1792,512]{1,0:T(8,128)S(1)} copy-done((f32[1792,512]{1,0:T(8,128)S(1)}, f32[1792,512]{1,0:T(8,128)}, u32[]{:S(2)}) %copy-start.13) | copy-done | bytes 3670040
  146.3 8.3 %shard_map.157 = (bf16[224,512]{1,0:T(8,128)(2,1)S(1)}, bf16[224,512]{1,0:T(8,128)(2,1)S(1)}, bf16[224,512]{1,0:T(8,128)(2,1)S(1)}, bf16[224,512]{1,0:T(8,128)(2...) custom-call(s32[9]{0:T(128)S(1)} %stack.115.refs_0_, ...), custom_call_target="tpu_custom_call" | custom-call | flops 3288334336 | bytes 3211264 | tf_op jit(solution)/shard_map/pallas_call | solution.py:202
  154.7 1.0 collective-permute-start.26
  156.4 1.5 collective-permute-start.22
  157.9 7.7 %collective-permute-start.21 = (bf16[448,512]{1,0:T(8,128)(2,1)S(1)}, bf16[448,512]{1,0:T(8,128)(2,1)S(1)}, u32[]{:S(2)}, u32[]{:S(2)}) collective-permute-start(bf16[448,512]{1,0:T(8,128)(2,1)S(1)} %get-tuple-element.11), channel_id=1, source_target_pairs={{0,0},{1,1},{2,2},{3,3},{4,4},{5,5},{6,6},{7,7},{8,8},{9,9},{10,10... | collective-permute-start | bytes 1376264 | tf_op jit(solution)/shard_map/ppermute | solution.py:38
  165.6 2.2 %collective-permute-start.24 = (bf16[224,512]{1,0:T(8,128)(2,1)S(1)}, bf16[224,512]{1,0:T(8,128)(2,1)S(1)}, u32[]{:S(2)}, u32[]{:S(2)}) collective-permute-start(bf16[224,512]{1,0:T(8,128)(2,1)S(1)} %get-tuple-element.14), channel_id=1, source_target_pairs={{0,3},{1,0},{2,1},{3,2},{4,7},{5,4},{6,5},{7,6},{8,11},{9,8},{10,9... | collective-permute-start | bytes 688136 | tf_op jit(solution)/shard_map/ppermute | solution.py:38
  167.9 1.4 collective-permute-start.25
  169.3 4.5 %collective-permute-start.27 = (bf16[224,512]{1,0:T(8,128)(2,1)S(1)}, bf16[224,512]{1,0:T(8,128)(2,1)S(1)}, u32[]{:S(2)}, u32[]{:S(2)}) collective-permute-start(bf16[224,512]{1,0:T(8,128)(2,1)S(1)} %add_convert_fusion), channel_id=1, source_target_pairs={{0,3},{1,0},{2,1},{3,2},{4,7},{5,4},{6,5},{7,6},{8,11},{9,8},{10,9... | collective-permute-start | bytes 688136 | tf_op jit(solution)/shard_map/ppermute | solution.py:38
  173.9 1.7 collective-permute-start.23
  175.7 7.4 %collective-permute-done.21 = bf16[448,512]{1,0:T(8,128)(2,1)S(1)} collective-permute-done((bf16[448,512]{1,0:T(8,128)(2,1)S(1)}, bf16[448,512]{1,0:T(8,128)(2,1)S(1)}, u32[]{:S(2)}, u32[]{:S(2)}) %collective-permute-start.21) | collective-permute-done | bytes 458784 | tf_op jit(solution)/shard_map/ppermute | solution.py:38
  183.2 0.1 convert_element_type.38
  183.3 6.9 %collective-permute-done.24 = bf16[224,512]{1,0:T(8,128)(2,1)S(1)} collective-permute-done((bf16[224,512]{1,0:T(8,128)(2,1)S(1)}, bf16[224,512]{1,0:T(8,128)(2,1)S(1)}, u32[]{:S(2)}, u32[]{:S(2)}) %collective-permute-start.24) | collective-permute-done | bytes 229408 | tf_op jit(solution)/shard_map/ppermute | solution.py:38
  190.2 2.5 %collective-permute-done.27 = bf16[224,512]{1,0:T(8,128)(2,1)S(1)} collective-permute-done((bf16[224,512]{1,0:T(8,128)(2,1)S(1)}, bf16[224,512]{1,0:T(8,128)(2,1)S(1)}, u32[]{:S(2)}, u32[]{:S(2)}) %collective-permute-start.27) | collective-permute-done | bytes 229408 | tf_op jit(solution)/shard_map/ppermute | solution.py:38
  192.7 0.2 fusion.14
  193.0 0.6 fusion.11
  193.7 0.3 copy-done.15
  194.0 0.1 copy-done.19
  194.2 0.2 collective-permute-start
  194.3 0.4 collective-permute-start.28
  194.8 0.7 collective-permute-done.30
  195.5 1.1 multiply_subtract_fusion
  196.6 0.2 collective-permute-done.28
  196.8 1.1 multiply_subtract_fusion.1
  (79 shorter events, 0.8 us)
Async XLA Ops:
  0.6 11.0 %collective-permute-start.7 = (bf16[112,1792]{1,0:T(8,128)(2,1)}, bf16[112,1792]{1,0:T(8,128)(2,1)S(1)}, u32[]{:S(2)}, u32[]{:S(2)}) collective-permute-start(bf16[112,1792]{1,0:T(8,128)(2,1)} %bitcast.61), channel_id=1, source_target_pairs={{0,0},{1,1},{2,2},{3,3},{4,4},{5,5},{6,6},{7,7},{8,8},{9,9},{10,10... | collective-permute-start | bytes 1204232 | tf_op jit(solution)/shard_map/ppermute | solution.py:38
  11.6 8.3 %collective-permute-start.8 = (bf16[112,1792]{1,0:T(8,128)(2,1)S(1)}, bf16[112,1792]{1,0:T(8,128)(2,1)S(1)}, u32[]{:S(2)}, u32[]{:S(2)}) collective-permute-start(bf16[112,1792]{1,0:T(8,128)(2,1)S(1)} %collective-permute-done.7), channel_id=1, source_target_pairs={{0,4},{1,5},{2,6},{3,7},{4,8},{5,9},{6,10},{7,11},{8,12},{9,13},{1... | collective-permute-start | bytes 1204232 | tf_op jit(solution)/shard_map/ppermute | solution.py:38
  12.9 7.1 %collective-permute-start.9 = (bf16[112,1792]{1,0:T(8,128)(2,1)S(1)}, bf16[112,1792]{1,0:T(8,128)(2,1)S(1)}, u32[]{:S(2)}, u32[]{:S(2)}) collective-permute-start(bf16[112,1792]{1,0:T(8,128)(2,1)S(1)} %collective-permute-done.7), channel_id=1, source_target_pairs={{0,12},{1,13},{2,14},{3,15},{4,0},{5,1},{6,2},{7,3},{8,4},{9,5},{1... | collective-permute-start | bytes 1204232 | tf_op jit(solution)/shard_map/ppermute | solution.py:38
  15.1 14.7 %copy-start.26 = (bf16[1,3584,256]{2,1,0:T(8,128)(2,1)S(1)}, bf16[1,3584,256]{2,1,0:T(8,128)(2,1)}, u32[]{:S(2)}) copy-start(bf16[1,3584,256]{2,1,0:T(8,128)(2,1)} %param.14) | copy-start | bytes 5505028
  15.1 22.8 %copy-start.16 = (f32[1,448,256]{2,1,0:T(8,128)S(1)}, f32[1,448,256]{2,1,0:T(8,128)}, u32[]{:S(2)}) copy-start(f32[1,448,256]{2,1,0:T(8,128)} %param.16) | copy-start | bytes 1376260
  19.9 5.9 %collective-permute-start.10 = (bf16[56,1792]{1,0:T(8,128)(2,1)S(1)}, bf16[56,1792]{1,0:T(8,128)(2,1)S(1)}, u32[]{:S(2)}, u32[]{:S(2)}) collective-permute-start(bf16[56,1792]{1,0:T(8,128)(2,1)S(1)} %slice.42), channel_id=1, source_target_pairs={{0,4},{1,5},{2,6},{3,7},{4,8},{5,9},{6,10},{7,11},{8,12},{9,13},{1... | collective-permute-start | bytes 602120 | tf_op jit(solution)/shard_map/ppermute | solution.py:38
  20.0 17.9 %copy-start.18 = (f32[1,448,256]{2,1,0:T(8,128)S(1)}, f32[1,448,256]{2,1,0:T(8,128)}, u32[]{:S(2)}) copy-start(f32[1,448,256]{2,1,0:T(8,128)} %param.15) | copy-start | bytes 1376260
  20.0 6.4 %collective-permute-start.11 = (bf16[56,1792]{1,0:T(8,128)(2,1)S(1)}, bf16[56,1792]{1,0:T(8,128)(2,1)S(1)}, u32[]{:S(2)}, u32[]{:S(2)}) collective-permute-start(bf16[56,1792]{1,0:T(8,128)(2,1)S(1)} %slice.43), channel_id=1, source_target_pairs={{0,12},{1,13},{2,14},{3,15},{4,0},{5,1},{6,2},{7,3},{8,4},{9,5},{1... | collective-permute-start | bytes 602120 | tf_op jit(solution)/shard_map/ppermute | solution.py:38
  27.2 50.1 %collective-permute-start.12 = (bf16[448,1792]{1,0:T(8,128)(2,1)}, bf16[448,1792]{1,0:T(8,128)(2,1)S(1)}, u32[]{:S(2)}, u32[]{:S(2)}) collective-permute-start(bf16[448,1792]{1,0:T(8,128)(2,1)} %constant_dynamic-update-slice_fusion.refs_7_), channel_id=1, source_target_pairs={{0,32},{1,33},{2,34},{3,35},{4,36},{5,37},{6,38},{7,39},{8,40},{9,... | collective-permute-start | bytes 4816904 | tf_op jit(solution)/shard_map/ppermute | solution.py:38
  29.2 48.6 %collective-permute-start.14 = (bf16[448,1792]{1,0:T(8,128)(2,1)}, bf16[448,1792]{1,0:T(8,128)(2,1)S(1)}, u32[]{:S(2)}, u32[]{:S(2)}) collective-permute-start(bf16[448,1792]{1,0:T(8,128)(2,1)} %constant_dynamic-update-slice_fusion.refs_7_), channel_id=1, source_target_pairs={{0,96},{1,97},{2,98},{3,99},{4,100},{5,101},{6,102},{7,103},{8,104... | collective-permute-start | bytes 4816904 | tf_op jit(solution)/shard_map/ppermute | solution.py:38
  29.9 73.9 %collective-permute-start.6 = (bf16[3584,256]{1,0:T(8,128)(2,1)S(1)}, bf16[3584,256]{1,0:T(8,128)(2,1)S(1)}, u32[]{:S(2)}, u32[]{:S(2)}) collective-permute-start(bf16[3584,256]{1,0:T(8,128)(2,1)S(1)} %bitcast.60), channel_id=1, source_target_pairs={{0,0},{1,1},{2,2},{3,3},{4,4},{5,5},{6,6},{7,7},{8,8},{9,9},{10,10... | collective-permute-start | bytes 5505032 | tf_op jit(solution)/shard_map/ppermute | solution.py:38
  38.0 24.9 %collective-permute-start.3 = (bf16[448,512]{1,0:T(8,128)(2,1)S(1)}, bf16[448,512]{1,0:T(8,128)(2,1)S(1)}, u32[]{:S(2)}, u32[]{:S(2)}) collective-permute-start(bf16[448,512]{1,0:T(8,128)(2,1)S(1)} %pad_maximum_fusion.1), channel_id=1, source_target_pairs={{0,1},{1,2},{2,3},{3,0},{4,5},{5,6},{6,7},{7,4},{8,9},{9,10},{10,1... | collective-permute-start | bytes 1376264 | tf_op jit(solution)/shard_map/ppermute | solution.py:38
  40.8 36.3 %collective-permute-start.2 = (bf16[448,512]{1,0:T(8,128)(2,1)S(1)}, bf16[448,512]{1,0:T(8,128)(2,1)S(1)}, u32[]{:S(2)}, u32[]{:S(2)}) collective-permute-start(bf16[448,512]{1,0:T(8,128)(2,1)S(1)} %pad_maximum_fusion.1), channel_id=1, source_target_pairs={{0,3},{1,0},{2,1},{3,2},{4,7},{5,4},{6,5},{7,6},{8,11},{9,8},{10,9... | collective-permute-start | bytes 1376264 | tf_op jit(solution)/shard_map/ppermute | solution.py:38
  63.0 24.5 %collective-permute-start.1 = (bf16[448,512]{1,0:T(8,128)(2,1)S(1)}, bf16[448,512]{1,0:T(8,128)(2,1)S(1)}, u32[]{:S(2)}, u32[]{:S(2)}) collective-permute-start(bf16[448,512]{1,0:T(8,128)(2,1)S(1)} %pad_maximum_fusion.1), channel_id=1, source_target_pairs={{0,0},{1,1},{2,2},{3,3},{4,4},{5,5},{6,6},{7,7},{8,8},{9,9},{10,10... | collective-permute-start | bytes 1376264 | tf_op jit(solution)/shard_map/ppermute | solution.py:38
  77.1 10.3 %copy-start.3 = (bf16[448,512]{1,0:T(8,128)(2,1)}, bf16[448,512]{1,0:T(8,128)(2,1)S(1)}, u32[]{:S(2)}) copy-start(bf16[448,512]{1,0:T(8,128)(2,1)S(1)} %collective-permute-done.2.refs_2_) | copy-start | bytes 1376260
  77.1 40.0 %collective-permute-start.18 = (bf16[448,1792]{1,0:T(8,128)(2,1)}, bf16[448,1792]{1,0:T(8,128)(2,1)}, u32[]{:S(2)}, u32[]{:S(2)}) collective-permute-start(bf16[448,1792]{1,0:T(8,128)(2,1)} %constant_dynamic-update-slice_fusion.refs_7_), channel_id=1, source_target_pairs={{0,128},{1,129},{2,130},{3,131},{4,132},{5,133},{6,134},{7,135},{8... | collective-permute-start | bytes 4816904 | tf_op jit(solution)/shard_map/ppermute | solution.py:38
  77.3 39.9 %collective-permute-start.19 = (bf16[448,1792]{1,0:T(8,128)(2,1)S(1)}, bf16[448,1792]{1,0:T(8,128)(2,1)}, u32[]{:S(2)}, u32[]{:S(2)}) collective-permute-start(bf16[448,1792]{1,0:T(8,128)(2,1)S(1)} %collective-permute-done.12.refs_9_), channel_id=1, source_target_pairs={{0,128},{1,129},{2,130},{3,131},{4,132},{5,133},{6,134},{7,135},{8... | collective-permute-start | bytes 4816904 | tf_op jit(solution)/shard_map/ppermute | solution.py:38
  77.7 39.4 %collective-permute-start.20 = (bf16[448,1792]{1,0:T(8,128)(2,1)S(1)}, bf16[448,1792]{1,0:T(8,128)(2,1)}, u32[]{:S(2)}, u32[]{:S(2)}) collective-permute-start(bf16[448,1792]{1,0:T(8,128)(2,1)S(1)} %collective-permute-done.14.refs_11_), channel_id=1, source_target_pairs={{0,128},{1,129},{2,130},{3,131},{4,132},{5,133},{6,134},{7,135},{8... | collective-permute-start | bytes 4816904 | tf_op jit(solution)/shard_map/ppermute | solution.py:38
  77.9 0.8 copy-start
  87.4 0.8 copy-start.9
  87.4 9.5 %collective-permute-start.4 = (bf16[224,512]{1,0:T(8,128)(2,1)S(1)}, bf16[224,512]{1,0:T(8,128)(2,1)S(1)}, u32[]{:S(2)}, u32[]{:S(2)}) collective-permute-start(bf16[224,512]{1,0:T(8,128)(2,1)S(1)} %slice.40), channel_id=1, source_target_pairs={{0,1},{1,2},{2,3},{3,0},{4,5},{5,6},{6,7},{7,4},{8,9},{9,10},{10,1... | collective-permute-start | bytes 688136 | tf_op jit(solution)/shard_map/ppermute | solution.py:38
  96.9 6.2 %collective-permute-start.5 = (bf16[224,512]{1,0:T(8,128)(2,1)S(1)}, bf16[224,512]{1,0:T(8,128)(2,1)S(1)}, u32[]{:S(2)}, u32[]{:S(2)}) collective-permute-start(bf16[224,512]{1,0:T(8,128)(2,1)S(1)} %slice.41), channel_id=1, source_target_pairs={{0,3},{1,0},{2,1},{3,2},{4,7},{5,4},{6,5},{7,6},{8,11},{9,8},{10,9... | collective-permute-start | bytes 688136 | tf_op jit(solution)/shard_map/ppermute | solution.py:38
  103.1 0.7 copy-start.11
  103.8 12.5 %collective-permute-start.13 = (bf16[224,1792]{1,0:T(8,128)(2,1)}, bf16[224,1792]{1,0:T(8,128)(2,1)}, u32[]{:S(2)}, u32[]{:S(2)}) collective-permute-start(bf16[224,1792]{1,0:T(8,128)(2,1)} %slice.44), channel_id=1, source_target_pairs={{0,32},{1,33},{2,34},{3,35},{4,36},{5,37},{6,38},{7,39},{8,40},{9,... | collective-permute-start | bytes 2408456 | tf_op jit(solution)/shard_map/ppermute | solution.py:38
  103.8 1.3 copy-start.6
  105.0 12.1 %collective-permute-start.15 = (bf16[224,1792]{1,0:T(8,128)(2,1)}, bf16[224,1792]{1,0:T(8,128)(2,1)}, u32[]{:S(2)}, u32[]{:S(2)}) collective-permute-start(bf16[224,1792]{1,0:T(8,128)(2,1)} %slice.45), channel_id=1, source_target_pairs={{0,96},{1,97},{2,98},{3,99},{4,100},{5,101},{6,102},{7,103},{8,104... | collective-permute-start | bytes 2408456 | tf_op jit(solution)/shard_map/ppermute | solution.py:38
  116.3 28.0 %collective-permute-start.16 = (bf16[224,1792]{1,0:T(8,128)(2,1)}, bf16[224,1792]{1,0:T(8,128)(2,1)S(1)}, u32[]{:S(2)}, u32[]{:S(2)}) collective-permute-start(bf16[224,1792]{1,0:T(8,128)(2,1)} %collective-permute-done.13.refs_7_), channel_id=1, source_target_pairs={{0,128},{1,129},{2,130},{3,131},{4,132},{5,133},{6,134},{7,135},{8... | collective-permute-start | bytes 2408456 | tf_op jit(solution)/shard_map/ppermute | solution.py:38
  117.1 27.1 %collective-permute-start.17 = (bf16[224,1792]{1,0:T(8,128)(2,1)}, bf16[224,1792]{1,0:T(8,128)(2,1)S(1)}, u32[]{:S(2)}, u32[]{:S(2)}) collective-permute-start(bf16[224,1792]{1,0:T(8,128)(2,1)} %collective-permute-done.15.refs_8_), channel_id=1, source_target_pairs={{0,128},{1,129},{2,130},{3,131},{4,132},{5,133},{6,134},{7,135},{8... | collective-permute-start | bytes 2408456 | tf_op jit(solution)/shard_map/ppermute | solution.py:38
  117.2 1.0 copy-start.1
  118.2 1.0 copy-start.4
  119.2 1.5 copy-start.7
  120.7 1.0 copy-start.10
  121.7 0.9 copy-start.12
  122.7 21.6 %copy-start.2 = (bf16[448,512]{1,0:T(8,128)(2,1)S(1)}, bf16[448,512]{1,0:T(8,128)(2,1)}, u32[]{:S(2)}) copy-start(bf16[448,512]{1,0:T(8,128)(2,1)} %copy-done) | copy-start | bytes 1376260
  122.7 21.6 %copy-start.5 = (bf16[448,512]{1,0:T(8,128)(2,1)S(1)}, bf16[448,512]{1,0:T(8,128)(2,1)}, u32[]{:S(2)}) copy-start(bf16[448,512]{1,0:T(8,128)(2,1)} %copy-done.3) | copy-start | bytes 1376260
  122.7 21.6 %copy-start.8 = (bf16[3584,256]{1,0:T(8,128)(2,1)S(1)}, bf16[3584,256]{1,0:T(8,128)(2,1)}, u32[]{:S(2)}) copy-start(bf16[3584,256]{1,0:T(8,128)(2,1)} %copy-done.6) | copy-start | bytes 5505028
  144.3 2.0 %copy-start.13 = (f32[1792,512]{1,0:T(8,128)S(1)}, f32[1792,512]{1,0:T(8,128)}, u32[]{:S(2)}) copy-start(f32[1792,512]{1,0:T(8,128)} %shard_map.156.refs_11_) | copy-start | bytes 11010052
  154.7 21.0 %copy-start.14 = (f32[448,256]{1,0:T(8,128)S(1)}, f32[448,256]{1,0:T(8,128)}, u32[]{:S(2)}) copy-start(f32[448,256]{1,0:T(8,128)} %param.22) | copy-start | bytes 1376260
  154.7 21.0 %copy-start.17 = (f32[1,448,256]{2,1,0:T(8,128)S(1)}, f32[1,448,256]{2,1,0:T(8,128)}, u32[]{:S(2)}) copy-start(f32[1,448,256]{2,1,0:T(8,128)} %param.16) | copy-start | bytes 1376260
  154.7 14.6 %collective-permute-start.26 = (bf16[224,512]{1,0:T(8,128)(2,1)S(1)}, bf16[224,512]{1,0:T(8,128)(2,1)S(1)}, u32[]{:S(2)}, u32[]{:S(2)}) collective-permute-start(bf16[224,512]{1,0:T(8,128)(2,1)S(1)} %get-tuple-element.17), channel_id=1, source_target_pairs={{0,3},{1,0},{2,1},{3,2},{4,7},{5,4},{6,5},{7,6},{8,11},{9,8},{10,9... | collective-permute-start | bytes 688136 | tf_op jit(solution)/shard_map/ppermute | solution.py:38
  156.4 17.5 %collective-permute-start.22 = (bf16[224,512]{1,0:T(8,128)(2,1)S(1)}, bf16[224,512]{1,0:T(8,128)(2,1)S(1)}, u32[]{:S(2)}, u32[]{:S(2)}) collective-permute-start(bf16[224,512]{1,0:T(8,128)(2,1)S(1)} %get-tuple-element.13), channel_id=1, source_target_pairs={{0,1},{1,2},{2,3},{3,0},{4,5},{5,6},{6,7},{7,4},{8,9},{9,10},{10,1... | collective-permute-start | bytes 688136 | tf_op jit(solution)/shard_map/ppermute | solution.py:38
  157.9 25.2 %collective-permute-start.21 = (bf16[448,512]{1,0:T(8,128)(2,1)S(1)}, bf16[448,512]{1,0:T(8,128)(2,1)S(1)}, u32[]{:S(2)}, u32[]{:S(2)}) collective-permute-start(bf16[448,512]{1,0:T(8,128)(2,1)S(1)} %get-tuple-element.11), channel_id=1, source_target_pairs={{0,0},{1,1},{2,2},{3,3},{4,4},{5,5},{6,6},{7,7},{8,8},{9,9},{10,10... | collective-permute-start | bytes 1376264 | tf_op jit(solution)/shard_map/ppermute | solution.py:38
  165.6 24.6 %collective-permute-start.24 = (bf16[224,512]{1,0:T(8,128)(2,1)S(1)}, bf16[224,512]{1,0:T(8,128)(2,1)S(1)}, u32[]{:S(2)}, u32[]{:S(2)}) collective-permute-start(bf16[224,512]{1,0:T(8,128)(2,1)S(1)} %get-tuple-element.14), channel_id=1, source_target_pairs={{0,3},{1,0},{2,1},{3,2},{4,7},{5,4},{6,5},{7,6},{8,11},{9,8},{10,9... | collective-permute-start | bytes 688136 | tf_op jit(solution)/shard_map/ppermute | solution.py:38
  167.9 22.4 %collective-permute-start.25 = (bf16[224,512]{1,0:T(8,128)(2,1)S(1)}, bf16[224,512]{1,0:T(8,128)(2,1)S(1)}, u32[]{:S(2)}, u32[]{:S(2)}) collective-permute-start(bf16[224,512]{1,0:T(8,128)(2,1)S(1)} %get-tuple-element.15), channel_id=1, source_target_pairs={{0,1},{1,2},{2,3},{3,0},{4,5},{5,6},{6,7},{7,4},{8,9},{9,10},{10,1... | collective-permute-start | bytes 688136 | tf_op jit(solution)/shard_map/ppermute | solution.py:38
  169.3 23.4 %collective-permute-start.27 = (bf16[224,512]{1,0:T(8,128)(2,1)S(1)}, bf16[224,512]{1,0:T(8,128)(2,1)S(1)}, u32[]{:S(2)}, u32[]{:S(2)}) collective-permute-start(bf16[224,512]{1,0:T(8,128)(2,1)S(1)} %add_convert_fusion), channel_id=1, source_target_pairs={{0,3},{1,0},{2,1},{3,2},{4,7},{5,4},{6,5},{7,6},{8,11},{9,8},{10,9... | collective-permute-start | bytes 688136 | tf_op jit(solution)/shard_map/ppermute | solution.py:38
  173.9 18.8 %collective-permute-start.23 = (bf16[224,512]{1,0:T(8,128)(2,1)S(1)}, bf16[224,512]{1,0:T(8,128)(2,1)S(1)}, u32[]{:S(2)}, u32[]{:S(2)}) collective-permute-start(bf16[224,512]{1,0:T(8,128)(2,1)S(1)} %add_convert_fusion.1), channel_id=1, source_target_pairs={{0,1},{1,2},{2,3},{3,0},{4,5},{5,6},{6,7},{7,4},{8,9},{9,10},{10,1... | collective-permute-start | bytes 688136 | tf_op jit(solution)/shard_map/ppermute | solution.py:38
  183.2 11.6 %collective-permute-start.29 = (f32[448,256]{1,0:T(8,128)S(1)}, f32[448,256]{1,0:T(8,128)S(1)}, u32[]{:S(2)}, u32[]{:S(2)}) collective-permute-start(f32[448,256]{1,0:T(8,128)S(1)} %bitcast_subtract_fusion), channel_id=1, source_target_pairs={{0,128},{1,129},{2,130},{3,131},{4,132},{5,133},{6,134},{7,135},{8... | collective-permute-start | bytes 1376264 | tf_op jit(solution)/shard_map/ppermute | solution.py:38
  183.3 9.6 %copy-start.22 = (f32[1,448,256]{2,1,0:T(8,128)S(1)}, f32[1,448,256]{2,1,0:T(8,128)}, u32[]{:S(2)}) copy-start(f32[1,448,256]{2,1,0:T(8,128)} %param.20) | copy-start | bytes 1376260
  183.3 9.6 %copy-start.23 = (f32[1,448,256]{2,1,0:T(8,128)S(1)}, f32[1,448,256]{2,1,0:T(8,128)}, u32[]{:S(2)}) copy-start(f32[1,448,256]{2,1,0:T(8,128)} %param.18) | copy-start | bytes 1376260
  183.3 9.6 %copy-start.24 = (f32[1,448,256]{2,1,0:T(8,128)S(1)}, f32[1,448,256]{2,1,0:T(8,128)}, u32[]{:S(2)}) copy-start(f32[1,448,256]{2,1,0:T(8,128)} %param.19) | copy-start | bytes 1376260
  183.3 9.6 %copy-start.25 = (f32[1,448,256]{2,1,0:T(8,128)S(1)}, f32[1,448,256]{2,1,0:T(8,128)}, u32[]{:S(2)}) copy-start(f32[1,448,256]{2,1,0:T(8,128)} %param.17) | copy-start | bytes 1376260
  192.9 1.0 copy-start.15
  192.9 1.1 copy-start.19
  193.5 1.9 copy-start.20
  193.6 1.9 collective-permute-start.30
  194.2 2.4 %collective-permute-start = (f32[448,256]{1,0:T(8,128)S(1)}, f32[448,256]{1,0:T(8,128)S(1)}, u32[]{:S(2)}, u32[]{:S(2)}) collective-permute-start(f32[448,256]{1,0:T(8,128)S(1)} %bitcast_subtract_fusion.1), channel_id=1, source_target_pairs={{0,128},{1,129},{2,130},{3,131},{4,132},{5,133},{6,134},{7,135},{8... | collective-permute-start | bytes 1376264 | tf_op jit(solution)/shard_map/ppermute | solution.py:38
  194.3 2.5 %copy-start.21 = (f32[448,256]{1,0:T(8,128)S(1)}, f32[448,256]{1,0:T(8,128)}, u32[]{:S(2)}) copy-start(f32[448,256]{1,0:T(8,128)} %param.23) | copy-start | bytes 1376260
  194.3 2.5 %collective-permute-start.28 = (f32[448,256]{1,0:T(8,128)S(1)}, f32[448,256]{1,0:T(8,128)S(1)}, u32[]{:S(2)}, u32[]{:S(2)}) collective-permute-start(f32[448,256]{1,0:T(8,128)S(1)} %get-tuple-element.23), channel_id=1, source_target_pairs={{0,128},{1,129},{2,130},{3,131},{4,132},{5,133},{6,134},{7,135},{8... | collective-permute-start | bytes 1376264 | tf_op jit(solution)/shard_map/ppermute | solution.py:38
